TPU v7x, 32 devices: a whole 2x2x4 slice. The times are simulated.
32 devices in a mesh: gz: 2 (over y), gy: 4 (over x, core), gx: 4 (over z).
Axes of the slice: x: 2, y: 2, z: 4, core: 2. Of those that a mesh axis runs over, the one named last changes fastest.
Arguments:
- labels: int32 [2, 32, 512], P('gz', 'gy', 'gx'), may hold values from 0 to 7
- tissue_tensors: float32 [6, 8], replicated, as said below
- electrodes: int32 [2, 64], replicated, may hold values from 0 to 32767, as said below
- initial: float32 [64, 2, 32, 512], P(None, 'gz', 'gy', 'gx'), may hold values from -4 to 4
Outputs:
- solution: float32 [64, 2, 32, 512], P(None, 'gz', 'gy', 'gx')
- residual: float32 [64, 2, 32, 512], P(None, 'gz', 'gy', 'gx')
Inputs may be any that keep to these rules, and one draw needn't show every extreme that they name: `tissue_tensors`: the tensors are symmetric and positive definite: each off-diagonal component is at most 0.3 times the geometric mean of its two diagonal components. `electrodes`: all 128 voxel indices are distinct; voxel (z, y, x) has index (z * 32 + y) * 512 + x.
All inputs are finite; a program needn't handle non-finite values.
Results may differ from a plain program's by a relative error of at most 0.0003.
Values sent between devices are 32-bit elements; how exact they have to be, the bound alone decides.
A program may use at most 64 MiB of HBM per device.

v0:
```python
import jax
import jax.numpy as jnp
from jax import lax
from jax.sharding import PartitionSpec as P

ITERS = 2


def from_behind(value, axis, steps):
    count = lax.axis_size(axis)
    initial, last = (max(0, -steps), min(count, count - steps))
    return lax.ppermute(value, axis, [(source, source + steps) for source in range(initial, last)])


def padded_2(block, sides, width):
    for axis, dim in sides:
        count = lax.axis_size(axis)
        forward = [(i, i + 1) for i in range(count - 1)]
        backward = [(target, source) for source, target in forward]
        low = lax.ppermute(
            lax.slice_in_dim(block, block.shape[dim] - width, None, axis=dim), axis, forward
        )
        high = lax.ppermute(lax.slice_in_dim(block, 0, width, axis=dim), axis, backward)
        block = jnp.concatenate([low, block, high], axis=dim)
    return block


def tensor_lookup(labels, table):
    result = jnp.zeros((6,) + labels.shape, jnp.float32)
    for tissue in range(table.shape[1]):
        result = result + jnp.where(
            labels[None] == tissue, table[:, tissue][:, None, None, None], jnp.float32(0.0)
        )
    return result


def flux_terms(tensor, grad_x, grad_y, grad_z):
    flux_x = tensor[0] * grad_x + tensor[3] * grad_y + tensor[4] * grad_z
    flux_y = tensor[3] * grad_x + tensor[1] * grad_y + tensor[5] * grad_z
    flux_z = tensor[4] * grad_x + tensor[5] * grad_y + tensor[2] * grad_z
    return (flux_x, flux_y, flux_z)


def lower_box(tensor):
    below_z = from_behind(tensor, "gz", 1)
    below_y = from_behind(tensor[:, :, -1:], "gy", 1)
    below_x = from_behind(tensor[:, :, :, -1:], "gx", 1)
    inner = jnp.concatenate([below_x, tensor], axis=3)
    side_y = jnp.pad(below_y, ((0, 0), (0, 0), (0, 0), (1, 0)))
    inner = jnp.concatenate([side_y, inner], axis=2)
    side_z = jnp.pad(below_z, ((0, 0), (0, 0), (1, 0), (1, 0)))
    return jnp.concatenate([side_z, inner], axis=1)


def operate_faces(direction, tensor_box):
    padded = padded_2(direction, (("gz", 1), ("gy", 2), ("gx", 3)), 1)
    centre = padded[:, :-1, :-1, :-1]
    grad_z = padded[:, 1:, :-1, :-1] - centre
    grad_y = padded[:, :-1, 1:, :-1] - centre
    grad_x = padded[:, :-1, :-1, 1:] - centre
    flux_x, flux_y, flux_z = flux_terms(tensor_box, grad_x, grad_y, grad_z)
    return (
        flux_z[:, :-1, 1:, 1:]
        - flux_z[:, 1:, 1:, 1:]
        + (flux_y[:, 1:, :-1, 1:] - flux_y[:, 1:, 1:, 1:])
        + (flux_x[:, 1:, 1:, :-1] - flux_x[:, 1:, 1:, 1:])
    )


def gram_of(first, second):
    leads = first.shape[0]
    return lax.dot_general(
        first.reshape(leads, -1),
        second.reshape(leads, -1),
        (((1,), (1,)), ((), ())),
        precision=lax.Precision.HIGHEST,
        preferred_element_type=jnp.float32,
    )


def combine_rows(coef, field):
    leads = field.shape[0]
    return jnp.dot(
        coef.T,
        field.reshape(leads, -1),
        precision=lax.Precision.HIGHEST,
        preferred_element_type=jnp.float32,
    ).reshape(field.shape)


def factor_solve(matrix, target):
    factor = jnp.linalg.cholesky(matrix)
    halfway = lax.linalg.triangular_solve(factor, target, left_side=True, lower=True)
    return lax.linalg.triangular_solve(
        factor, halfway, left_side=True, lower=True, transpose_a=True
    )


def body(labels, tissue_tensors, electrodes, initial):
    cells_z, cells_y, cells_x = labels.shape
    rows_all = cells_y * lax.axis_size("gy")
    cols_all = cells_x * lax.axis_size("gx")
    depth_ids = lax.axis_index("gz") * cells_z + lax.broadcasted_iota(jnp.int32, labels.shape, 0)
    row_ids = lax.axis_index("gy") * cells_y + lax.broadcasted_iota(jnp.int32, labels.shape, 1)
    col_ids = lax.axis_index("gx") * cells_x + lax.broadcasted_iota(jnp.int32, labels.shape, 2)
    voxel_id = (depth_ids * rows_all + row_ids) * cols_all + col_ids
    sources = (voxel_id[None] == electrodes[0][:, None, None, None]).astype(jnp.float32) - (
        voxel_id[None] == electrodes[1][:, None, None, None]
    ).astype(jnp.float32)
    tensor = tensor_lookup(labels, tissue_tensors)
    tensor_box = lower_box(tensor)

    def operate(field):
        return operate_faces(field, tensor_box)

    solution = initial
    residual = sources - operate(initial)
    direction = residual
    rr_now = lax.psum(gram_of(residual, residual), ("gz", "gy", "gx"))
    for iteration in range(ITERS):
        image = operate(direction)
        curve = lax.psum(gram_of(direction, image), ("gz", "gy", "gx"))
        step_coef = factor_solve(curve, rr_now)
        solution = solution + combine_rows(step_coef, direction)
        residual = residual - combine_rows(step_coef, image)
        if iteration + 1 < ITERS:
            rr_next = lax.psum(gram_of(residual, residual), ("gz", "gy", "gx"))
            beta_coef = factor_solve(rr_now, rr_next)
            direction = residual + combine_rows(beta_coef, direction)
            rr_now = rr_next
    return (solution, residual)


def solution(mesh):
    placed = (P("gz", "gy", "gx"), P(), P(), P(None, "gz", "gy", "gx"))
    return jax.shard_map(
        body,
        mesh=mesh,
        in_specs=placed,
        out_specs=(P(None, "gz", "gy", "gx"), P(None, "gz", "gy", "gx")),
        check_vma=False,
    )
```

profile of v0, /device:TPU:0, one launch (start us, length us, event | category | flops | bytes accessed | tf_op | source)
XLA Modules:
  0.0 279.7 jit_solution(1200948065979888118)
XLA Ops:
  1.7 4.9 %collective-permute-start.3 = (f32[64,1,8,128]{3,0,2,1:T(8,128)S(1)}, f32[64,1,8,128]{3,0,2,1:T(8,128)S(1)}, u32[]{:S(2)}, u32[]{:S(2)}) collective-permute-start(f32[64,1,8,128]{3,0,2,1:T(8,128)S(1)} %copy.64), channel_id=1, source_target_pairs={{0,16},{1,17},{2,18},{3,19},{4,20},{5,21},{6,22},{7,23},{8,24},{9,... | collective-permute-start | bytes 786440 | tf_op jit(solution)/shard_map/ppermute | solution.py:20
  10.0 4.6 %collective-permute-start = (f32[6,1,8,128]{3,2,1,0:T(8,128)S(1)}, f32[6,1,8,128]{3,2,1,0:T(8,128)S(1)}, u32[]{:S(2)}, u32[]{:S(2)}) collective-permute-start(f32[6,1,8,128]{3,2,1,0:T(8,128)S(1)} %select_add_fusion), channel_id=1, source_target_pairs={{0,16},{1,17},{2,18},{3,19},{4,20},{5,21},{6,22},{7,23},{8,24},{9,... | collective-permute-start | bytes 73736 | tf_op jit(solution)/shard_map/ppermute | solution.py:12
  14.6 3.5 %collective-permute-start.2 = (f32[6,1,8,1]{3,2,1,0:T(8,128)S(1)}, f32[6,1,8,1]{3,2,1,0:T(8,128)S(1)}, u32[]{:S(2)}, u32[]{:S(2)}) collective-permute-start(f32[6,1,8,1]{3,2,1,0:T(8,128)S(1)} %slice.282), channel_id=1, source_target_pairs={{0,1},{1,2},{2,3},{4,5},{5,6},{6,7},{8,9},{9,10},{10,11},{12,13},{... | collective-permute-start | bytes 584 | tf_op jit(solution)/shard_map/ppermute | solution.py:12
  20.4 4.1 %collective-permute-start.5 = (f32[64,3,1,128]{3,0,2,1:T(8,128)S(1)}, f32[64,3,1,128]{3,0,2,1:T(8,128)S(1)}, u32[]{:S(2)}, u32[]{:S(2)}) collective-permute-start(f32[64,3,1,128]{3,0,2,1:T(8,128)S(1)} %get-tuple-element.43), channel_id=1, source_target_pairs={{0,4},{4,8},{8,12},{1,5},{5,9},{9,13},{2,6},{6,10},{10,14},{3,7},{... | collective-permute-start | bytes 294920 | tf_op jit(solution)/shard_map/ppermute | solution.py:20
  29.2 3.5 %collective-permute-start.8 = (f32[64,3,10,1]{0,3,2,1:T(1,128)}, f32[64,3,10,1]{0,3,2,1:T(1,128)S(1)}, u32[]{:S(2)}, u32[]{:S(2)}) collective-permute-start(f32[64,3,10,1]{0,3,2,1:T(1,128)} %copy.52), channel_id=1, source_target_pairs={{0,1},{1,2},{2,3},{4,5},{5,6},{6,7},{8,9},{9,10},{10,11},{12,13},{... | collective-permute-start | bytes 23048 | tf_op jit(solution)/shard_map/ppermute | solution.py:20
  44.5 4.6 %collective-permute-start.9 = (f32[64,1,8,128]{3,0,2,1:T(8,128)S(1)}, f32[64,1,8,128]{3,0,2,1:T(8,128)S(1)}, u32[]{:S(2)}, u32[]{:S(2)}) collective-permute-start(f32[64,1,8,128]{3,0,2,1:T(8,128)S(1)} %fusion.21), channel_id=1, source_target_pairs={{0,16},{1,17},{2,18},{3,19},{4,20},{5,21},{6,22},{7,23},{8,24},{9,... | collective-permute-start | bytes 786440 | tf_op jit(solution)/shard_map/ppermute | solution.py:20
  49.1 4.9 %collective-permute-done.10 = f32[64,1,8,128]{3,0,2,1:T(8,128)S(1)} collective-permute-done((f32[64,1,8,128]{3,0,2,1:T(8,128)S(1)}, f32[64,1,8,128]{3,0,2,1:T(8,128)S(1)}, u32[]{:S(2)}, u32[]{:S(2)}) %collective-permute-start.10) | collective-permute-done | bytes 262176 | tf_op jit(solution)/shard_map/ppermute | solution.py:23
  55.7 2.2 collective-permute-start.11
  61.8 3.4 %collective-permute-start.14 = (f32[64,3,10,1]{0,3,2,1:T(1,128)S(1)}, f32[64,3,10,1]{0,3,2,1:T(1,128)S(1)}, u32[]{:S(2)}, u32[]{:S(2)}) collective-permute-start(f32[64,3,10,1]{0,3,2,1:T(1,128)S(1)} %copy.56), channel_id=1, source_target_pairs={{0,1},{1,2},{2,3},{4,5},{5,6},{6,7},{8,9},{9,10},{10,11},{12,13},{... | collective-permute-start | bytes 23048 | tf_op jit(solution)/shard_map/ppermute | solution.py:20
  73.3 2.0 copy.55
  78.5 42.6 %all-reduce.2 = (f32[64,64]{0,1:T(8,128)S(1)}, f32[64,64]{0,1:T(8,128)S(1)}) all-reduce(f32[64,64]{0,1:T(8,128)S(1)} %copy-done.22, f32[64,64]{0,1:T(8,128)S(1)} %convolution_bitcast_fusion.11), channel_id=1, replica_groups=mesh['gz'=2,'gy'=4,'gx'=4] {'gz','gy','gx'}, use_global_device_ids=true, to_apply=%region_3.5 | all-reduce | flops 8192 | bytes 65536 | tf_op jit(solution)/shard_map/psum | solution.py:119
  121.3 5.8 %cholesky.70 = f32[64,64]{1,0:T(8,128)S(1)} custom-call(f32[64,64]{1,0:T(8,128)S(1)} %get-tuple-element.61), custom_call_target="Cholesky" | custom-call | tf_op jit(solution)/shard_map/jit(cholesky)/cholesky | solution.py:92
  128.5 4.9 %custom-call.15 = f32[1,64,64]{1,2,0:T(8,128)S(1)} custom-call(f32[1,64,64]{2,1,0:T(8,128)S(1)} %fusion.34), custom_call_target="InvertDiagBlocksLowerTriangular" | custom-call | tf_op jit(solution)/shard_map/triangular_solve/custom-call.2 | solution.py:94
  133.4 5.9 %cholesky.59 = f32[64,64]{1,0:T(8,128)S(1)} custom-call(f32[64,64]{1,0:T(8,128)S(1)} %get-tuple-element.62), custom_call_target="Cholesky" | custom-call | tf_op jit(solution)/shard_map/jit(cholesky)/cholesky | solution.py:92
  140.6 4.9 %custom-call.13 = f32[1,64,64]{1,2,0:T(8,128)S(1)} custom-call(f32[1,64,64]{2,1,0:T(8,128)S(1)} %fusion.33), custom_call_target="InvertDiagBlocksLowerTriangular" | custom-call | tf_op jit(solution)/shard_map/triangular_solve/custom-call.2 | solution.py:94
  146.8 38.9 %psum.30 = f32[64,64]{1,0:T(8,128)S(1)} all-reduce(f32[64,64]{1,0:T(8,128)S(1)} %convolution_bitcast_fusion.9), channel_id=1, replica_groups=mesh['gz'=2,'gy'=4,'gx'=4] {'gz','gy','gx'}, use_global_device_ids=true, to_apply=%region_4.8 | all-reduce | flops 4096 | bytes 32768 | tf_op jit(solution)/shard_map/psum | solution.py:127
  186.6 4.2 %collective-permute-start.15 = (f32[64,1,8,128]{3,0,2,1:T(8,128)S(1)}, f32[64,1,8,128]{3,0,2,1:T(8,128)S(1)}, u32[]{:S(2)}, u32[]{:S(2)}) collective-permute-start(f32[64,1,8,128]{3,0,2,1:T(8,128)S(1)} %fusion.6), channel_id=1, source_target_pairs={{0,16},{1,17},{2,18},{3,19},{4,20},{5,21},{6,22},{7,23},{8,24},{9,... | collective-permute-start | bytes 786440 | tf_op jit(solution)/shard_map/ppermute | solution.py:20
  192.2 3.9 %collective-permute-done.15 = f32[64,1,8,128]{3,0,2,1:T(8,128)S(1)} collective-permute-done((f32[64,1,8,128]{3,0,2,1:T(8,128)S(1)}, f32[64,1,8,128]{3,0,2,1:T(8,128)S(1)}, u32[]{:S(2)}, u32[]{:S(2)}) %collective-permute-start.15) | collective-permute-done | bytes 262176 | tf_op jit(solution)/shard_map/ppermute | solution.py:20
  196.0 4.1 %collective-permute-done.16 = f32[64,1,8,128]{3,0,2,1:T(8,128)S(1)} collective-permute-done((f32[64,1,8,128]{3,0,2,1:T(8,128)S(1)}, f32[64,1,8,128]{3,0,2,1:T(8,128)S(1)}, u32[]{:S(2)}, u32[]{:S(2)}) %collective-permute-start.16) | collective-permute-done | bytes 262176 | tf_op jit(solution)/shard_map/ppermute | solution.py:23
  202.8 2.9 %collective-permute-done.18 = f32[64,3,1,128]{3,0,2,1:T(8,128)S(1)} collective-permute-done((f32[64,3,1,128]{3,0,2,1:T(8,128)S(1)}, f32[64,3,1,128]{3,0,2,1:T(8,128)S(1)}, u32[]{:S(2)}, u32[]{:S(2)}) %collective-permute-start.18) | collective-permute-done | bytes 98336 | tf_op jit(solution)/shard_map/ppermute | solution.py:23
  207.2 3.3 %collective-permute-start.20 = (f32[64,3,10,1]{0,3,2,1:T(1,128)S(1)}, f32[64,3,10,1]{0,3,2,1:T(1,128)S(1)}, u32[]{:S(2)}, u32[]{:S(2)}) collective-permute-start(f32[64,3,10,1]{0,3,2,1:T(1,128)S(1)} %copy.73), channel_id=1, source_target_pairs={{0,1},{1,2},{2,3},{4,5},{5,6},{6,7},{8,9},{9,10},{10,11},{12,13},{... | collective-permute-start | bytes 23048 | tf_op jit(solution)/shard_map/ppermute | solution.py:20
  223.5 40.5 %psum.31 = f32[64,64]{0,1:T(8,128)S(1)} all-reduce(f32[64,64]{0,1:T(8,128)S(1)} %convolution_bitcast_fusion.8), channel_id=1, replica_groups=mesh['gz'=2,'gy'=4,'gx'=4] {'gz','gy','gx'}, use_global_device_ids=true, to_apply=%region_5.9 | all-reduce | flops 4096 | bytes 32768 | tf_op jit(solution)/shard_map/psum | solution.py:122
  264.1 5.8 %cholesky.81 = f32[64,64]{1,0:T(8,128)S(1)} custom-call(f32[64,64]{1,0:T(8,128)S(1)} %fusion.39), custom_call_target="Cholesky" | custom-call | tf_op jit(solution)/shard_map/jit(cholesky)/cholesky | solution.py:92
  271.3 4.9 %custom-call.17 = f32[1,64,64]{1,2,0:T(8,128)S(1)} custom-call(f32[1,64,64]{2,1,0:T(8,128)S(1)} %fusion.35), custom_call_target="InvertDiagBlocksLowerTriangular" | custom-call | tf_op jit(solution)/shard_map/triangular_solve/custom-call.2 | solution.py:94
  (156 shorter events, 67.9 us)
Async XLA Ops:
  1.7 18.6 %collective-permute-start.3 = (f32[64,1,8,128]{3,0,2,1:T(8,128)S(1)}, f32[64,1,8,128]{3,0,2,1:T(8,128)S(1)}, u32[]{:S(2)}, u32[]{:S(2)}) collective-permute-start(f32[64,1,8,128]{3,0,2,1:T(8,128)S(1)} %copy.64), channel_id=1, source_target_pairs={{0,16},{1,17},{2,18},{3,19},{4,20},{5,21},{6,22},{7,23},{8,24},{9,... | collective-permute-start | bytes 786440 | tf_op jit(solution)/shard_map/ppermute | solution.py:20
  6.6 13.8 %collective-permute-start.4 = (f32[64,1,8,128]{3,0,2,1:T(8,128)S(1)}, f32[64,1,8,128]{3,0,2,1:T(8,128)S(1)}, u32[]{:S(2)}, u32[]{:S(2)}) collective-permute-start(f32[64,1,8,128]{3,0,2,1:T(8,128)S(1)} %copy.64), channel_id=1, source_target_pairs={{16,0},{17,1},{18,2},{19,3},{20,4},{21,5},{22,6},{23,7},{24,8},{25... | collective-permute-start | bytes 786440 | tf_op jit(solution)/shard_map/ppermute | solution.py:23
  10.0 15.9 %collective-permute-start = (f32[6,1,8,128]{3,2,1,0:T(8,128)S(1)}, f32[6,1,8,128]{3,2,1,0:T(8,128)S(1)}, u32[]{:S(2)}, u32[]{:S(2)}) collective-permute-start(f32[6,1,8,128]{3,2,1,0:T(8,128)S(1)} %select_add_fusion), channel_id=1, source_target_pairs={{0,16},{1,17},{2,18},{3,19},{4,20},{5,21},{6,22},{7,23},{8,24},{9,... | collective-permute-start | bytes 73736 | tf_op jit(solution)/shard_map/ppermute | solution.py:12
  14.6 11.2 %collective-permute-start.2 = (f32[6,1,8,1]{3,2,1,0:T(8,128)S(1)}, f32[6,1,8,1]{3,2,1,0:T(8,128)S(1)}, u32[]{:S(2)}, u32[]{:S(2)}) collective-permute-start(f32[6,1,8,1]{3,2,1,0:T(8,128)S(1)} %slice.282), channel_id=1, source_target_pairs={{0,1},{1,2},{2,3},{4,5},{5,6},{6,7},{8,9},{9,10},{10,11},{12,13},{... | collective-permute-start | bytes 584 | tf_op jit(solution)/shard_map/ppermute | solution.py:12
  18.1 7.8 %collective-permute-start.1 = (f32[6,1,1,128]{3,2,1,0:T(1,128)S(1)}, f32[6,1,1,128]{3,2,1,0:T(1,128)S(1)}, u32[]{:S(2)}, u32[]{:S(2)}) collective-permute-start(f32[6,1,1,128]{3,2,1,0:T(1,128)S(1)} %slice.281), channel_id=1, source_target_pairs={{0,4},{4,8},{8,12},{1,5},{5,9},{9,13},{2,6},{6,10},{10,14},{3,7},{... | collective-permute-start | bytes 9224 | tf_op jit(solution)/shard_map/ppermute | solution.py:12
  20.4 5.6 %collective-permute-start.5 = (f32[64,3,1,128]{3,0,2,1:T(8,128)S(1)}, f32[64,3,1,128]{3,0,2,1:T(8,128)S(1)}, u32[]{:S(2)}, u32[]{:S(2)}) collective-permute-start(f32[64,3,1,128]{3,0,2,1:T(8,128)S(1)} %get-tuple-element.43), channel_id=1, source_target_pairs={{0,4},{4,8},{8,12},{1,5},{5,9},{9,13},{2,6},{6,10},{10,14},{3,7},{... | collective-permute-start | bytes 294920 | tf_op jit(solution)/shard_map/ppermute | solution.py:20
  24.6 3.2 %collective-permute-start.6 = (f32[64,3,1,128]{3,0,2,1:T(8,128)S(1)}, f32[64,3,1,128]{3,0,2,1:T(8,128)S(1)}, u32[]{:S(2)}, u32[]{:S(2)}) collective-permute-start(f32[64,3,1,128]{3,0,2,1:T(8,128)S(1)} %get-tuple-element.44), channel_id=1, source_target_pairs={{4,0},{8,4},{12,8},{5,1},{9,5},{13,9},{6,2},{10,6},{14,10},{7,3},{... | collective-permute-start | bytes 294920 | tf_op jit(solution)/shard_map/ppermute | solution.py:23
  29.2 5.8 %collective-permute-start.8 = (f32[64,3,10,1]{0,3,2,1:T(1,128)}, f32[64,3,10,1]{0,3,2,1:T(1,128)S(1)}, u32[]{:S(2)}, u32[]{:S(2)}) collective-permute-start(f32[64,3,10,1]{0,3,2,1:T(1,128)} %copy.52), channel_id=1, source_target_pairs={{0,1},{1,2},{2,3},{4,5},{5,6},{6,7},{8,9},{9,10},{10,11},{12,13},{... | collective-permute-start | bytes 23048 | tf_op jit(solution)/shard_map/ppermute | solution.py:20
  33.3 43.5 %copy-start.3 = (f32[2,9,129]{2,1,0:T(8,128)}, f32[2,9,129]{2,1,0:T(8,128)S(1)}, u32[]{:S(2)}) copy-start(f32[2,9,129]{2,1,0:T(8,128)S(1)} %get-tuple-element.50) | copy-start | bytes 27868
  33.6 5.6 %collective-permute-start.7 = (f32[64,3,10,1]{0,3,2,1:T(1,128)S(1)}, f32[64,3,10,1]{0,3,2,1:T(1,128)S(1)}, u32[]{:S(2)}, u32[]{:S(2)}) collective-permute-start(f32[64,3,10,1]{0,3,2,1:T(1,128)S(1)} %copy.50), channel_id=1, source_target_pairs={{1,0},{2,1},{3,2},{5,4},{6,5},{7,6},{9,8},{10,9},{11,10},{13,12},{... | collective-permute-start | bytes 23048 | tf_op jit(solution)/shard_map/ppermute | solution.py:23
  43.2 10.8 %collective-permute-start.10 = (f32[64,1,8,128]{3,0,2,1:T(8,128)S(1)}, f32[64,1,8,128]{3,0,2,1:T(8,128)S(1)}, u32[]{:S(2)}, u32[]{:S(2)}) collective-permute-start(f32[64,1,8,128]{3,0,2,1:T(8,128)S(1)} %fusion.21), channel_id=1, source_target_pairs={{16,0},{17,1},{18,2},{19,3},{20,4},{21,5},{22,6},{23,7},{24,8},{25... | collective-permute-start | bytes 786440 | tf_op jit(solution)/shard_map/ppermute | solution.py:23
  44.5 11.2 %collective-permute-start.9 = (f32[64,1,8,128]{3,0,2,1:T(8,128)S(1)}, f32[64,1,8,128]{3,0,2,1:T(8,128)S(1)}, u32[]{:S(2)}, u32[]{:S(2)}) collective-permute-start(f32[64,1,8,128]{3,0,2,1:T(8,128)S(1)} %fusion.21), channel_id=1, source_target_pairs={{0,16},{1,17},{2,18},{3,19},{4,20},{5,21},{6,22},{7,23},{8,24},{9,... | collective-permute-start | bytes 786440 | tf_op jit(solution)/shard_map/ppermute | solution.py:20
  55.7 3.5 %collective-permute-start.11 = (f32[64,3,1,128]{3,0,2,1:T(8,128)S(1)}, f32[64,3,1,128]{3,0,2,1:T(8,128)S(1)}, u32[]{:S(2)}, u32[]{:S(2)}) collective-permute-start(f32[64,3,1,128]{3,0,2,1:T(8,128)S(1)} %get-tuple-element.41), channel_id=1, source_target_pairs={{0,4},{4,8},{8,12},{1,5},{5,9},{9,13},{2,6},{6,10},{10,14},{3,7},{... | collective-permute-start | bytes 294920 | tf_op jit(solution)/shard_map/ppermute | solution.py:20
  57.9 3.2 %collective-permute-start.12 = (f32[64,3,1,128]{3,0,2,1:T(8,128)S(1)}, f32[64,3,1,128]{3,0,2,1:T(8,128)S(1)}, u32[]{:S(2)}, u32[]{:S(2)}) collective-permute-start(f32[64,3,1,128]{3,0,2,1:T(8,128)S(1)} %get-tuple-element.42), channel_id=1, source_target_pairs={{4,0},{8,4},{12,8},{5,1},{9,5},{13,9},{6,2},{10,6},{14,10},{7,3},{... | collective-permute-start | bytes 294920 | tf_op jit(solution)/shard_map/ppermute | solution.py:23
  61.8 6.8 %collective-permute-start.14 = (f32[64,3,10,1]{0,3,2,1:T(1,128)S(1)}, f32[64,3,10,1]{0,3,2,1:T(1,128)S(1)}, u32[]{:S(2)}, u32[]{:S(2)}) collective-permute-start(f32[64,3,10,1]{0,3,2,1:T(1,128)S(1)} %copy.56), channel_id=1, source_target_pairs={{0,1},{1,2},{2,3},{4,5},{5,6},{6,7},{8,9},{9,10},{10,11},{12,13},{... | collective-permute-start | bytes 23048 | tf_op jit(solution)/shard_map/ppermute | solution.py:20
  67.3 5.9 %collective-permute-start.13 = (f32[64,3,10,1]{0,3,2,1:T(1,128)}, f32[64,3,10,1]{0,3,2,1:T(1,128)}, u32[]{:S(2)}, u32[]{:S(2)}) collective-permute-start(f32[64,3,10,1]{0,3,2,1:T(1,128)} %copy.54), channel_id=1, source_target_pairs={{1,0},{2,1},{3,2},{5,4},{6,5},{7,6},{9,8},{10,9},{11,10},{13,12},{... | collective-permute-start | bytes 23048 | tf_op jit(solution)/shard_map/ppermute | solution.py:23
  186.6 9.4 %collective-permute-start.15 = (f32[64,1,8,128]{3,0,2,1:T(8,128)S(1)}, f32[64,1,8,128]{3,0,2,1:T(8,128)S(1)}, u32[]{:S(2)}, u32[]{:S(2)}) collective-permute-start(f32[64,1,8,128]{3,0,2,1:T(8,128)S(1)} %fusion.6), channel_id=1, source_target_pairs={{0,16},{1,17},{2,18},{3,19},{4,20},{5,21},{6,22},{7,23},{8,24},{9,... | collective-permute-start | bytes 786440 | tf_op jit(solution)/shard_map/ppermute | solution.py:20
  190.9 9.3 %collective-permute-start.16 = (f32[64,1,8,128]{3,0,2,1:T(8,128)S(1)}, f32[64,1,8,128]{3,0,2,1:T(8,128)S(1)}, u32[]{:S(2)}, u32[]{:S(2)}) collective-permute-start(f32[64,1,8,128]{3,0,2,1:T(8,128)S(1)} %fusion.6), channel_id=1, source_target_pairs={{16,0},{17,1},{18,2},{19,3},{20,4},{21,5},{22,6},{23,7},{24,8},{25... | collective-permute-start | bytes 786440 | tf_op jit(solution)/shard_map/ppermute | solution.py:23
  200.2 2.6 collective-permute-start.17
  201.5 4.3 %collective-permute-start.18 = (f32[64,3,1,128]{3,0,2,1:T(8,128)S(1)}, f32[64,3,1,128]{3,0,2,1:T(8,128)S(1)}, u32[]{:S(2)}, u32[]{:S(2)}) collective-permute-start(f32[64,3,1,128]{3,0,2,1:T(8,128)S(1)} %get-tuple-element.40), channel_id=1, source_target_pairs={{4,0},{8,4},{12,8},{5,1},{9,5},{13,9},{6,2},{10,6},{14,10},{7,3},{... | collective-permute-start | bytes 294920 | tf_op jit(solution)/shard_map/ppermute | solution.py:23
  207.2 6.4 %collective-permute-start.20 = (f32[64,3,10,1]{0,3,2,1:T(1,128)S(1)}, f32[64,3,10,1]{0,3,2,1:T(1,128)S(1)}, u32[]{:S(2)}, u32[]{:S(2)}) collective-permute-start(f32[64,3,10,1]{0,3,2,1:T(1,128)S(1)} %copy.73), channel_id=1, source_target_pairs={{0,1},{1,2},{2,3},{4,5},{5,6},{6,7},{8,9},{9,10},{10,11},{12,13},{... | collective-permute-start | bytes 23048 | tf_op jit(solution)/shard_map/ppermute | solution.py:20
  212.3 5.9 %collective-permute-start.19 = (f32[64,3,10,1]{0,3,2,1:T(1,128)}, f32[64,3,10,1]{0,3,2,1:T(1,128)}, u32[]{:S(2)}, u32[]{:S(2)}) collective-permute-start(f32[64,3,10,1]{0,3,2,1:T(1,128)} %copy.71), channel_id=1, source_target_pairs={{1,0},{2,1},{3,2},{5,4},{6,5},{7,6},{9,8},{10,9},{11,10},{13,12},{... | collective-permute-start | bytes 23048 | tf_op jit(solution)/shard_map/ppermute | solution.py:23
  222.6 53.6 %copy-start.21 = (f32[64,64]{1,0:T(8,128)S(1)}, f32[64,64]{1,0:T(8,128)}, u32[]{:S(2)}) copy-start(f32[64,64]{1,0:T(8,128)} %copy-done.20) | copy-start | bytes 49156
  223.4 54.6 %copy-start.5 = (f32[64,1,8,128]{3,2,0,1:T(8,128)S(1)}, f32[64,1,8,128]{3,2,0,1:T(8,128)}, u32[]{:S(2)}) copy-start(f32[64,1,8,128]{3,2,0,1:T(8,128)} %copy.77) | copy-start | bytes 786436
  (20 other events, 159.4 us)
where the time goes:
time: 281 us; the launch traced here: 280 us
  blocking collectives  122 us (43%)
  starting transfers between devices  52.4 us (19%)
  other arithmetic  50.7 us (18%)
  waiting for transfers between devices  25.3 us (9%)
  local copies, waits for them, and re-layouts  22.4 us (8%)
  matrix products  5.49 us (2%)
    psum x1, blocking collectives, body(): rr_now = lax.psum(gram_of(residual, residual), ('gz', 'gy', 'gx'))  42.6 us
    psum x1, blocking collectives, body(): curve = lax.psum(gram_of(direction, image), ('gz', 'gy', 'gx'))  40.5 us
    psum x1, blocking collectives, body(): rr_next = lax.psum(gram_of(residual, residual), ('gz', 'gy', 'gx'))  38.9 us
    ppermute x9, starting transfers between devices, padded_2(): lax.ppermute(lax.slice_in_dim(block, block.shape[dim] - width, None, axis...  31.5 us
    ppermute x9, waiting for transfers between devices, padded_2(): lax.ppermute(lax.slice_in_dim(block, 0, width, axis=dim), axis, backward)  19.7 us
    another operation x9, other arithmetic, factor_solve(): factor = jnp.linalg.cholesky(matrix)  19.6 us
    another operation x6, other arithmetic, factor_solve(): lax.linalg.triangular_solve(factor, halfway, left_side=True, lower=True,...  16.6 us
    ppermute x9, starting transfers between devices, padded_2(): lax.ppermute(lax.slice_in_dim(block, 0, width, axis=dim), axis, backward)  11.6 us
  transfers between devices with their start and end apart: 21, of which 10 were waited for; matrix products, arithmetic and copies ran while one was open for 6% of the time, Pallas kernels for 0%

commit v1 on v0

--- a/solution.py
+++ b/solution.py
@@ -124,7 +124,7 @@
         solution = solution + combine_rows(step_coef, direction)
         residual = residual - combine_rows(step_coef, image)
         if iteration + 1 < ITERS:
-            rr_next = lax.psum(gram_of(residual, residual), ("gz", "gy", "gx"))
+            rr_next = lax.psum(lax.psum(gram_of(residual, residual), ("gy", "gx")), "gz")
             beta_coef = factor_solve(rr_now, rr_next)
             direction = residual + combine_rows(beta_coef, direction)
             rr_now = rr_next

time: 281 us -> 306 us (1.089)
  blocking collectives: 122 us -> 151 us
  starting transfers between devices: 52.4 us -> 48.6 us
    psum x1 -> x2, blocking collectives: 38.9 us -> 67.6 us  [the longest x1 58.7 us: body(): lax.psum(gram_of(residual, residual), ('gy', 'gx'))]
    ppermute x9, starting transfers between devices: 31.5 us -> 27.7 us  [padded_2(): lax.ppermute(lax.slice_in_dim(block, block.shape[dim] - width, None, axis...]
where the time goes in v1:
time: 306 us; the launch traced here: 305 us
  blocking collectives  151 us (49%)
  other arithmetic  50.7 us (17%)
  starting transfers between devices  48.6 us (16%)
  waiting for transfers between devices  25.5 us (8%)
  local copies, waits for them, and re-layouts  22.4 us (7%)
  matrix products  5.49 us (2%)
    psum x1, blocking collectives, body(): lax.psum(gram_of(residual, residual), ('gy', 'gx'))  58.7 us
    psum x1, blocking collectives, body(): rr_now = lax.psum(gram_of(residual, residual), ('gz', 'gy', 'gx'))  42.6 us
    psum x1, blocking collectives, body(): curve = lax.psum(gram_of(direction, image), ('gz', 'gy', 'gx'))  40.4 us
    ppermute x9, starting transfers between devices, padded_2(): lax.ppermute(lax.slice_in_dim(block, block.shape[dim] - width, None, axis...  27.7 us
    ppermute x9, waiting for transfers between devices, padded_2(): lax.ppermute(lax.slice_in_dim(block, 0, width, axis=dim), axis, backward)  21.2 us
    another operation x9, other arithmetic, factor_solve(): factor = jnp.linalg.cholesky(matrix)  19.6 us
    another operation x6, other arithmetic, factor_solve(): lax.linalg.triangular_solve(factor, halfway, left_side=True, lower=True,...  16.6 us
    ppermute x9, starting transfers between devices, padded_2(): lax.ppermute(lax.slice_in_dim(block, 0, width, axis=dim), axis, backward)  11.6 us
  transfers between devices with their start and end apart: 21, of which 10 were waited for; matrix products, arithmetic and copies ran while one was open for 6% of the time, Pallas kernels for 0%

profile of v1, /device:TPU:0, one launch (start us, length us, event | category | flops | bytes accessed | tf_op | source)
XLA Modules:
  0.0 304.7 jit_solution(1585819785310053116)
XLA Ops:
  1.7 4.9 %collective-permute-start.3 = (f32[64,1,8,128]{3,0,2,1:T(8,128)S(1)}, f32[64,1,8,128]{3,0,2,1:T(8,128)S(1)}, u32[]{:S(2)}, u32[]{:S(2)}) collective-permute-start(f32[64,1,8,128]{3,0,2,1:T(8,128)S(1)} %copy.64), channel_id=1, source_target_pairs={{0,16},{1,17},{2,18},{3,19},{4,20},{5,21},{6,22},{7,23},{8,24},{9,... | collective-permute-start | bytes 786440 | tf_op jit(solution)/shard_map/ppermute | solution.py:20
  10.0 4.6 %collective-permute-start = (f32[6,1,8,128]{3,2,1,0:T(8,128)S(1)}, f32[6,1,8,128]{3,2,1,0:T(8,128)S(1)}, u32[]{:S(2)}, u32[]{:S(2)}) collective-permute-start(f32[6,1,8,128]{3,2,1,0:T(8,128)S(1)} %select_add_fusion), channel_id=1, source_target_pairs={{0,16},{1,17},{2,18},{3,19},{4,20},{5,21},{6,22},{7,23},{8,24},{9,... | collective-permute-start | bytes 73736 | tf_op jit(solution)/shard_map/ppermute | solution.py:12
  14.6 3.5 %collective-permute-start.2 = (f32[6,1,8,1]{3,2,1,0:T(8,128)S(1)}, f32[6,1,8,1]{3,2,1,0:T(8,128)S(1)}, u32[]{:S(2)}, u32[]{:S(2)}) collective-permute-start(f32[6,1,8,1]{3,2,1,0:T(8,128)S(1)} %slice.282), channel_id=1, source_target_pairs={{0,1},{1,2},{2,3},{4,5},{5,6},{6,7},{8,9},{9,10},{10,11},{12,13},{... | collective-permute-start | bytes 584 | tf_op jit(solution)/shard_map/ppermute | solution.py:12
  20.4 4.1 %collective-permute-start.5 = (f32[64,3,1,128]{3,0,2,1:T(8,128)S(1)}, f32[64,3,1,128]{3,0,2,1:T(8,128)S(1)}, u32[]{:S(2)}, u32[]{:S(2)}) collective-permute-start(f32[64,3,1,128]{3,0,2,1:T(8,128)S(1)} %get-tuple-element.43), channel_id=1, source_target_pairs={{0,4},{4,8},{8,12},{1,5},{5,9},{9,13},{2,6},{6,10},{10,14},{3,7},{... | collective-permute-start | bytes 294920 | tf_op jit(solution)/shard_map/ppermute | solution.py:20
  29.2 3.5 %collective-permute-start.8 = (f32[64,3,10,1]{0,3,2,1:T(1,128)}, f32[64,3,10,1]{0,3,2,1:T(1,128)S(1)}, u32[]{:S(2)}, u32[]{:S(2)}) collective-permute-start(f32[64,3,10,1]{0,3,2,1:T(1,128)} %copy.52), channel_id=1, source_target_pairs={{0,1},{1,2},{2,3},{4,5},{5,6},{6,7},{8,9},{9,10},{10,11},{12,13},{... | collective-permute-start | bytes 23048 | tf_op jit(solution)/shard_map/ppermute | solution.py:20
  44.5 4.6 %collective-permute-start.9 = (f32[64,1,8,128]{3,0,2,1:T(8,128)S(1)}, f32[64,1,8,128]{3,0,2,1:T(8,128)S(1)}, u32[]{:S(2)}, u32[]{:S(2)}) collective-permute-start(f32[64,1,8,128]{3,0,2,1:T(8,128)S(1)} %fusion.21), channel_id=1, source_target_pairs={{0,16},{1,17},{2,18},{3,19},{4,20},{5,21},{6,22},{7,23},{8,24},{9,... | collective-permute-start | bytes 786440 | tf_op jit(solution)/shard_map/ppermute | solution.py:20
  49.1 4.9 %collective-permute-done.10 = f32[64,1,8,128]{3,0,2,1:T(8,128)S(1)} collective-permute-done((f32[64,1,8,128]{3,0,2,1:T(8,128)S(1)}, f32[64,1,8,128]{3,0,2,1:T(8,128)S(1)}, u32[]{:S(2)}, u32[]{:S(2)}) %collective-permute-start.10) | collective-permute-done | bytes 262176 | tf_op jit(solution)/shard_map/ppermute | solution.py:23
  55.7 2.2 collective-permute-start.11
  61.8 3.4 %collective-permute-start.14 = (f32[64,3,10,1]{0,3,2,1:T(1,128)S(1)}, f32[64,3,10,1]{0,3,2,1:T(1,128)S(1)}, u32[]{:S(2)}, u32[]{:S(2)}) collective-permute-start(f32[64,3,10,1]{0,3,2,1:T(1,128)S(1)} %copy.56), channel_id=1, source_target_pairs={{0,1},{1,2},{2,3},{4,5},{5,6},{6,7},{8,9},{9,10},{10,11},{12,13},{... | collective-permute-start | bytes 23048 | tf_op jit(solution)/shard_map/ppermute | solution.py:20
  73.3 2.0 copy.55
  78.5 42.6 %all-reduce.2 = (f32[64,64]{0,1:T(8,128)S(1)}, f32[64,64]{0,1:T(8,128)S(1)}) all-reduce(f32[64,64]{0,1:T(8,128)S(1)} %copy-done.22, f32[64,64]{0,1:T(8,128)S(1)} %convolution_bitcast_fusion.11), channel_id=1, replica_groups=mesh['gz'=2,'gy'=4,'gx'=4] {'gz','gy','gx'}, use_global_device_ids=true, to_apply=%region_3.5 | all-reduce | flops 8192 | bytes 65536 | tf_op jit(solution)/shard_map/psum | solution.py:119
  121.3 5.8 %cholesky.70 = f32[64,64]{1,0:T(8,128)S(1)} custom-call(f32[64,64]{1,0:T(8,128)S(1)} %get-tuple-element.61), custom_call_target="Cholesky" | custom-call | tf_op jit(solution)/shard_map/jit(cholesky)/cholesky | solution.py:92
  128.5 4.9 %custom-call.15 = f32[1,64,64]{1,2,0:T(8,128)S(1)} custom-call(f32[1,64,64]{2,1,0:T(8,128)S(1)} %fusion.34), custom_call_target="InvertDiagBlocksLowerTriangular" | custom-call | tf_op jit(solution)/shard_map/triangular_solve/custom-call.2 | solution.py:94
  133.4 5.9 %cholesky.59 = f32[64,64]{1,0:T(8,128)S(1)} custom-call(f32[64,64]{1,0:T(8,128)S(1)} %get-tuple-element.62), custom_call_target="Cholesky" | custom-call | tf_op jit(solution)/shard_map/jit(cholesky)/cholesky | solution.py:92
  140.6 4.9 %custom-call.13 = f32[1,64,64]{1,2,0:T(8,128)S(1)} custom-call(f32[1,64,64]{2,1,0:T(8,128)S(1)} %fusion.33), custom_call_target="InvertDiagBlocksLowerTriangular" | custom-call | tf_op jit(solution)/shard_map/triangular_solve/custom-call.2 | solution.py:94
  146.8 58.7 %psum.37 = f32[64,64]{1,0:T(8,128)S(1)} all-reduce(f32[64,64]{1,0:T(8,128)S(1)} %convolution_bitcast_fusion.9), channel_id=1, replica_groups=mesh['gz'=2,'gy'=4,'gx'=4] {'gy','gx'}, use_global_device_ids=true, to_apply=%region_4.8 | all-reduce | flops 4096 | bytes 32768 | tf_op jit(solution)/shard_map/psum | solution.py:127
  205.5 8.9 %psum.38 = f32[64,64]{1,0:T(8,128)S(1)} all-reduce(f32[64,64]{1,0:T(8,128)S(1)} %psum.37), channel_id=1, replica_groups=mesh['gz'=2,'gy'=4,'gx'=4] {'gz'}, use_global_device_ids=true, to_apply=%region_5.9 | all-reduce | flops 4096 | bytes 32768 | tf_op jit(solution)/shard_map/psum | solution.py:127
  218.7 2.6 collective-permute-done.15
  221.2 4.4 %collective-permute-done.16 = f32[64,1,8,128]{3,0,2,1:T(8,128)S(1)} collective-permute-done((f32[64,1,8,128]{3,0,2,1:T(8,128)S(1)}, f32[64,1,8,128]{3,0,2,1:T(8,128)S(1)}, u32[]{:S(2)}, u32[]{:S(2)}) %collective-permute-start.16) | collective-permute-done | bytes 262176 | tf_op jit(solution)/shard_map/ppermute | solution.py:23
  228.3 4.1 %collective-permute-done.18 = f32[64,3,1,128]{3,0,2,1:T(8,128)S(1)} collective-permute-done((f32[64,3,1,128]{3,0,2,1:T(8,128)S(1)}, f32[64,3,1,128]{3,0,2,1:T(8,128)S(1)}, u32[]{:S(2)}, u32[]{:S(2)}) %collective-permute-start.18) | collective-permute-done | bytes 98336 | tf_op jit(solution)/shard_map/ppermute | solution.py:23
  243.3 2.0 copy.72
  248.6 40.4 %psum.39 = f32[64,64]{0,1:T(8,128)S(1)} all-reduce(f32[64,64]{0,1:T(8,128)S(1)} %convolution_bitcast_fusion.8), channel_id=1, replica_groups=mesh['gz'=2,'gy'=4,'gx'=4] {'gz','gy','gx'}, use_global_device_ids=true, to_apply=%region_6.10 | all-reduce | flops 4096 | bytes 32768 | tf_op jit(solution)/shard_map/psum | solution.py:122
  289.1 5.8 %cholesky.81 = f32[64,64]{1,0:T(8,128)S(1)} custom-call(f32[64,64]{1,0:T(8,128)S(1)} %fusion.39), custom_call_target="Cholesky" | custom-call | tf_op jit(solution)/shard_map/jit(cholesky)/cholesky | solution.py:92
  296.3 4.9 %custom-call.17 = f32[1,64,64]{1,2,0:T(8,128)S(1)} custom-call(f32[1,64,64]{2,1,0:T(8,128)S(1)} %fusion.35), custom_call_target="InvertDiagBlocksLowerTriangular" | custom-call | tf_op jit(solution)/shard_map/triangular_solve/custom-call.2 | solution.py:94
  (157 shorter events, 69.6 us)
Async XLA Ops:
  1.7 18.6 %collective-permute-start.3 = (f32[64,1,8,128]{3,0,2,1:T(8,128)S(1)}, f32[64,1,8,128]{3,0,2,1:T(8,128)S(1)}, u32[]{:S(2)}, u32[]{:S(2)}) collective-permute-start(f32[64,1,8,128]{3,0,2,1:T(8,128)S(1)} %copy.64), channel_id=1, source_target_pairs={{0,16},{1,17},{2,18},{3,19},{4,20},{5,21},{6,22},{7,23},{8,24},{9,... | collective-permute-start | bytes 786440 | tf_op jit(solution)/shard_map/ppermute | solution.py:20
  6.6 13.8 %collective-permute-start.4 = (f32[64,1,8,128]{3,0,2,1:T(8,128)S(1)}, f32[64,1,8,128]{3,0,2,1:T(8,128)S(1)}, u32[]{:S(2)}, u32[]{:S(2)}) collective-permute-start(f32[64,1,8,128]{3,0,2,1:T(8,128)S(1)} %copy.64), channel_id=1, source_target_pairs={{16,0},{17,1},{18,2},{19,3},{20,4},{21,5},{22,6},{23,7},{24,8},{25... | collective-permute-start | bytes 786440 | tf_op jit(solution)/shard_map/ppermute | solution.py:23
  10.0 15.9 %collective-permute-start = (f32[6,1,8,128]{3,2,1,0:T(8,128)S(1)}, f32[6,1,8,128]{3,2,1,0:T(8,128)S(1)}, u32[]{:S(2)}, u32[]{:S(2)}) collective-permute-start(f32[6,1,8,128]{3,2,1,0:T(8,128)S(1)} %select_add_fusion), channel_id=1, source_target_pairs={{0,16},{1,17},{2,18},{3,19},{4,20},{5,21},{6,22},{7,23},{8,24},{9,... | collective-permute-start | bytes 73736 | tf_op jit(solution)/shard_map/ppermute | solution.py:12
  14.6 11.2 %collective-permute-start.2 = (f32[6,1,8,1]{3,2,1,0:T(8,128)S(1)}, f32[6,1,8,1]{3,2,1,0:T(8,128)S(1)}, u32[]{:S(2)}, u32[]{:S(2)}) collective-permute-start(f32[6,1,8,1]{3,2,1,0:T(8,128)S(1)} %slice.282), channel_id=1, source_target_pairs={{0,1},{1,2},{2,3},{4,5},{5,6},{6,7},{8,9},{9,10},{10,11},{12,13},{... | collective-permute-start | bytes 584 | tf_op jit(solution)/shard_map/ppermute | solution.py:12
  18.1 7.8 %collective-permute-start.1 = (f32[6,1,1,128]{3,2,1,0:T(1,128)S(1)}, f32[6,1,1,128]{3,2,1,0:T(1,128)S(1)}, u32[]{:S(2)}, u32[]{:S(2)}) collective-permute-start(f32[6,1,1,128]{3,2,1,0:T(1,128)S(1)} %slice.281), channel_id=1, source_target_pairs={{0,4},{4,8},{8,12},{1,5},{5,9},{9,13},{2,6},{6,10},{10,14},{3,7},{... | collective-permute-start | bytes 9224 | tf_op jit(solution)/shard_map/ppermute | solution.py:12
  20.4 5.6 %collective-permute-start.5 = (f32[64,3,1,128]{3,0,2,1:T(8,128)S(1)}, f32[64,3,1,128]{3,0,2,1:T(8,128)S(1)}, u32[]{:S(2)}, u32[]{:S(2)}) collective-permute-start(f32[64,3,1,128]{3,0,2,1:T(8,128)S(1)} %get-tuple-element.43), channel_id=1, source_target_pairs={{0,4},{4,8},{8,12},{1,5},{5,9},{9,13},{2,6},{6,10},{10,14},{3,7},{... | collective-permute-start | bytes 294920 | tf_op jit(solution)/shard_map/ppermute | solution.py:20
  24.6 3.2 %collective-permute-start.6 = (f32[64,3,1,128]{3,0,2,1:T(8,128)S(1)}, f32[64,3,1,128]{3,0,2,1:T(8,128)S(1)}, u32[]{:S(2)}, u32[]{:S(2)}) collective-permute-start(f32[64,3,1,128]{3,0,2,1:T(8,128)S(1)} %get-tuple-element.44), channel_id=1, source_target_pairs={{4,0},{8,4},{12,8},{5,1},{9,5},{13,9},{6,2},{10,6},{14,10},{7,3},{... | collective-permute-start | bytes 294920 | tf_op jit(solution)/shard_map/ppermute | solution.py:23
  29.2 5.8 %collective-permute-start.8 = (f32[64,3,10,1]{0,3,2,1:T(1,128)}, f32[64,3,10,1]{0,3,2,1:T(1,128)S(1)}, u32[]{:S(2)}, u32[]{:S(2)}) collective-permute-start(f32[64,3,10,1]{0,3,2,1:T(1,128)} %copy.52), channel_id=1, source_target_pairs={{0,1},{1,2},{2,3},{4,5},{5,6},{6,7},{8,9},{9,10},{10,11},{12,13},{... | collective-permute-start | bytes 23048 | tf_op jit(solution)/shard_map/ppermute | solution.py:20
  33.6 5.6 %collective-permute-start.7 = (f32[64,3,10,1]{0,3,2,1:T(1,128)S(1)}, f32[64,3,10,1]{0,3,2,1:T(1,128)S(1)}, u32[]{:S(2)}, u32[]{:S(2)}) collective-permute-start(f32[64,3,10,1]{0,3,2,1:T(1,128)S(1)} %copy.50), channel_id=1, source_target_pairs={{1,0},{2,1},{3,2},{5,4},{6,5},{7,6},{9,8},{10,9},{11,10},{13,12},{... | collective-permute-start | bytes 23048 | tf_op jit(solution)/shard_map/ppermute | solution.py:23
  43.2 10.8 %collective-permute-start.10 = (f32[64,1,8,128]{3,0,2,1:T(8,128)S(1)}, f32[64,1,8,128]{3,0,2,1:T(8,128)S(1)}, u32[]{:S(2)}, u32[]{:S(2)}) collective-permute-start(f32[64,1,8,128]{3,0,2,1:T(8,128)S(1)} %fusion.21), channel_id=1, source_target_pairs={{16,0},{17,1},{18,2},{19,3},{20,4},{21,5},{22,6},{23,7},{24,8},{25... | collective-permute-start | bytes 786440 | tf_op jit(solution)/shard_map/ppermute | solution.py:23
  44.5 11.2 %collective-permute-start.9 = (f32[64,1,8,128]{3,0,2,1:T(8,128)S(1)}, f32[64,1,8,128]{3,0,2,1:T(8,128)S(1)}, u32[]{:S(2)}, u32[]{:S(2)}) collective-permute-start(f32[64,1,8,128]{3,0,2,1:T(8,128)S(1)} %fusion.21), channel_id=1, source_target_pairs={{0,16},{1,17},{2,18},{3,19},{4,20},{5,21},{6,22},{7,23},{8,24},{9,... | collective-permute-start | bytes 786440 | tf_op jit(solution)/shard_map/ppermute | solution.py:20
  55.7 3.5 %collective-permute-start.11 = (f32[64,3,1,128]{3,0,2,1:T(8,128)S(1)}, f32[64,3,1,128]{3,0,2,1:T(8,128)S(1)}, u32[]{:S(2)}, u32[]{:S(2)}) collective-permute-start(f32[64,3,1,128]{3,0,2,1:T(8,128)S(1)} %get-tuple-element.41), channel_id=1, source_target_pairs={{0,4},{4,8},{8,12},{1,5},{5,9},{9,13},{2,6},{6,10},{10,14},{3,7},{... | collective-permute-start | bytes 294920 | tf_op jit(solution)/shard_map/ppermute | solution.py:20
  57.9 3.2 %collective-permute-start.12 = (f32[64,3,1,128]{3,0,2,1:T(8,128)S(1)}, f32[64,3,1,128]{3,0,2,1:T(8,128)S(1)}, u32[]{:S(2)}, u32[]{:S(2)}) collective-permute-start(f32[64,3,1,128]{3,0,2,1:T(8,128)S(1)} %get-tuple-element.42), channel_id=1, source_target_pairs={{4,0},{8,4},{12,8},{5,1},{9,5},{13,9},{6,2},{10,6},{14,10},{7,3},{... | collective-permute-start | bytes 294920 | tf_op jit(solution)/shard_map/ppermute | solution.py:23
  61.8 6.8 %collective-permute-start.14 = (f32[64,3,10,1]{0,3,2,1:T(1,128)S(1)}, f32[64,3,10,1]{0,3,2,1:T(1,128)S(1)}, u32[]{:S(2)}, u32[]{:S(2)}) collective-permute-start(f32[64,3,10,1]{0,3,2,1:T(1,128)S(1)} %copy.56), channel_id=1, source_target_pairs={{0,1},{1,2},{2,3},{4,5},{5,6},{6,7},{8,9},{9,10},{10,11},{12,13},{... | collective-permute-start | bytes 23048 | tf_op jit(solution)/shard_map/ppermute | solution.py:20
  67.4 5.9 %collective-permute-start.13 = (f32[64,3,10,1]{0,3,2,1:T(1,128)}, f32[64,3,10,1]{0,3,2,1:T(1,128)}, u32[]{:S(2)}, u32[]{:S(2)}) collective-permute-start(f32[64,3,10,1]{0,3,2,1:T(1,128)} %copy.54), channel_id=1, source_target_pairs={{1,0},{2,1},{3,2},{5,4},{6,5},{7,6},{9,8},{10,9},{11,10},{13,12},{... | collective-permute-start | bytes 23048 | tf_op jit(solution)/shard_map/ppermute | solution.py:23
  146.0 69.4 %copy-start.18 = (f32[64,64,1]{0,1,2:T(8,128)}, f32[64,64,1]{0,1,2:T(8,128)S(1)}, u32[]{:S(2)}) copy-start(f32[64,64,1]{0,1,2:T(8,128)S(1)} %convolution_bitcast_fusion.7) | copy-start | bytes 49156
  215.4 5.8 %collective-permute-start.15 = (f32[64,1,8,128]{3,0,2,1:T(8,128)S(1)}, f32[64,1,8,128]{3,0,2,1:T(8,128)S(1)}, u32[]{:S(2)}, u32[]{:S(2)}) collective-permute-start(f32[64,1,8,128]{3,0,2,1:T(8,128)S(1)} %fusion.6), channel_id=1, source_target_pairs={{0,16},{1,17},{2,18},{3,19},{4,20},{5,21},{6,22},{7,23},{8,24},{9,... | collective-permute-start | bytes 786440 | tf_op jit(solution)/shard_map/ppermute | solution.py:20
  217.4 8.3 %collective-permute-start.16 = (f32[64,1,8,128]{3,0,2,1:T(8,128)S(1)}, f32[64,1,8,128]{3,0,2,1:T(8,128)S(1)}, u32[]{:S(2)}, u32[]{:S(2)}) collective-permute-start(f32[64,1,8,128]{3,0,2,1:T(8,128)S(1)} %fusion.6), channel_id=1, source_target_pairs={{16,0},{17,1},{18,2},{19,3},{20,4},{21,5},{22,6},{23,7},{24,8},{25... | collective-permute-start | bytes 786440 | tf_op jit(solution)/shard_map/ppermute | solution.py:23
  225.6 2.6 collective-permute-start.17
  227.0 5.5 %collective-permute-start.18 = (f32[64,3,1,128]{3,0,2,1:T(8,128)S(1)}, f32[64,3,1,128]{3,0,2,1:T(8,128)S(1)}, u32[]{:S(2)}, u32[]{:S(2)}) collective-permute-start(f32[64,3,1,128]{3,0,2,1:T(8,128)S(1)} %get-tuple-element.40), channel_id=1, source_target_pairs={{4,0},{8,4},{12,8},{5,1},{9,5},{13,9},{6,2},{10,6},{14,10},{7,3},{... | collective-permute-start | bytes 294920 | tf_op jit(solution)/shard_map/ppermute | solution.py:23
  233.8 4.9 %collective-permute-start.20 = (f32[64,3,10,1]{0,3,2,1:T(1,128)S(1)}, f32[64,3,10,1]{0,3,2,1:T(1,128)S(1)}, u32[]{:S(2)}, u32[]{:S(2)}) collective-permute-start(f32[64,3,10,1]{0,3,2,1:T(1,128)S(1)} %copy.73), channel_id=1, source_target_pairs={{0,1},{1,2},{2,3},{4,5},{5,6},{6,7},{8,9},{9,10},{10,11},{12,13},{... | collective-permute-start | bytes 23048 | tf_op jit(solution)/shard_map/ppermute | solution.py:20
  237.4 5.9 %collective-permute-start.19 = (f32[64,3,10,1]{0,3,2,1:T(1,128)}, f32[64,3,10,1]{0,3,2,1:T(1,128)}, u32[]{:S(2)}, u32[]{:S(2)}) collective-permute-start(f32[64,3,10,1]{0,3,2,1:T(1,128)} %copy.71), channel_id=1, source_target_pairs={{1,0},{2,1},{3,2},{5,4},{6,5},{7,6},{9,8},{10,9},{11,10},{13,12},{... | collective-permute-start | bytes 23048 | tf_op jit(solution)/shard_map/ppermute | solution.py:23
  247.7 53.6 %copy-start.21 = (f32[64,64]{1,0:T(8,128)S(1)}, f32[64,64]{1,0:T(8,128)}, u32[]{:S(2)}) copy-start(f32[64,64]{1,0:T(8,128)} %copy-done.20) | copy-start | bytes 49156
  248.5 54.6 %copy-start.5 = (f32[64,1,8,128]{3,2,0,1:T(8,128)S(1)}, f32[64,1,8,128]{3,2,0,1:T(8,128)}, u32[]{:S(2)}) copy-start(f32[64,1,8,128]{3,2,0,1:T(8,128)} %copy.77) | copy-start | bytes 786436
  (20 other events, 163.5 us)
